TPU v7x, 256 devices: a whole 4x4x8 slice. The times are simulated.
256 devices in a mesh: tm: 8 (over x, y_hi), rows: 32 (over z, y_lo, core).
Axes of the slice: x: 4, y: 4 (y_hi: 2, y_lo: 2; y = y_hi * 2 + y_lo), z: 8, core: 2. Of those that a mesh axis runs over, the one named last changes fastest.
Arguments:
- queries: bfloat16 [16, 64, 96, 1024], P('tm', 'rows'), may hold values from -5 to 5
- keys: bfloat16 [16, 64, 96, 1024], P('tm', 'rows'), may hold values from -5 to 5
- values: bfloat16 [16, 64, 96, 1024], P('tm', 'rows'), may hold values from -5 to 5
- window_lists: int32 [256, 12], replicated, may hold values from -1 to 255, as said below
Outputs:
- attended: bfloat16 [16, 64, 96, 1024], P('tm', 'rows')
Inputs may be any that keep to these rules, and one draw needn't show every extreme that they name: `window_lists`: each row lists distinct tiles whose frame-tile, row-tile and column-tile indices each differ from the row's own tile by at most one; the tile itself is always listed; listed ids come first, then -1; some row lists 12 tiles.
All inputs are finite; a program needn't handle non-finite values.
Results may differ from a plain program's by a relative error of at most 0.0047.
Values may be sent and summed in bfloat16 or wider, within the bound.
A program may use at most 64 MiB of HBM per device.

v0:
```python
import jax
import jax.numpy as jnp
from jax import lax
from jax.sharding import PartitionSpec as P

HEADS = 8
TILE_H = 8
TILE_COLS = 4


def swapped(shard, axis, bit):
    return lax.ppermute(shard, axis, [(i, i ^ 1 << bit) for i in range(lax.axis_size(axis))])


def shifted(block, axis, distance):
    devices = range(lax.axis_size(axis))
    route = [(i - distance, i) for i in devices if i - distance in devices]
    return lax.ppermute(block, axis, route)


def split_heads(block):
    place = lax.axis_index("rows")
    for level in range(HEADS.bit_length() - 1):
        mine = place >> level & 1
        heads_now = block.shape[0]
        paired = block.reshape((heads_now // 2, 2) + block.shape[1:])
        staying = lax.dynamic_index_in_dim(paired, mine, 1, keepdims=False)
        leaving = lax.dynamic_index_in_dim(paired, 1 - mine, 1, keepdims=False)
        arrived = swapped(leaving, "rows", level)
        lower = jnp.where(mine == 0, staying, arrived)
        upper = jnp.where(mine == 0, arrived, staying)
        block = jnp.concatenate((lower, upper), axis=1)
    return block


def merge_heads(block):
    place = lax.axis_index("rows")
    for level in reversed(range(HEADS.bit_length() - 1)):
        mine = place >> level & 1
        heads_now = block.shape[0]
        slab_count = block.shape[1]
        halves = block.reshape((heads_now, 2, slab_count // 2) + block.shape[2:])
        staying = lax.dynamic_index_in_dim(halves, mine, 1, keepdims=False)
        leaving = lax.dynamic_index_in_dim(halves, 1 - mine, 1, keepdims=False)
        arrived = swapped(leaving, "rows", level)
        lower = jnp.where(mine == 0, staying, arrived)
        upper = jnp.where(mine == 0, arrived, staying)
        block = jnp.stack((lower, upper), axis=1).reshape(
            (heads_now * 2, slab_count // 2) + block.shape[2:]
        )
    return block


def body(queries, keys, values, window_lists):
    frames, rows_dev, width, feat = queries.shape
    head_dim = feat // HEADS
    stacked = jnp.stack((queries, keys, values), 0).reshape(
        3, frames, rows_dev, width, HEADS, head_dim
    )
    stacked = jnp.transpose(stacked, (4, 0, 1, 2, 3, 5))[:, None]
    gathered = split_heads(stacked)[0]
    slabs = gathered.shape[0]
    group_rows = slabs * rows_dev
    local = jnp.transpose(gathered, (1, 2, 0, 3, 4, 5)).reshape(
        3, frames, group_rows, width, head_dim
    )
    query_part = local[0]
    key_value = local[1:]
    below = shifted(key_value[:, :, group_rows - TILE_H :], "rows", slabs)
    above = shifted(key_value[:, :, :TILE_H], "rows", -slabs)
    column = jnp.concatenate((below, key_value, above), axis=2)
    earlier = shifted(column, "tm", 1)
    later = shifted(column, "tm", -1)
    window = jnp.stack((earlier, column, later), 0)
    tile_w = width // TILE_COLS
    stack_rows = group_rows // TILE_H + 2
    own_rows = group_rows // TILE_H
    tiled = window.reshape(3, 2, frames, stack_rows, TILE_H, TILE_COLS, tile_w, head_dim)
    tiled = jnp.transpose(tiled, (1, 0, 3, 5, 2, 4, 6, 7))
    tiled = tiled.reshape(2, 3 * stack_rows * TILE_COLS, frames * TILE_H * tile_w, head_dim)
    key_tiles = tiled[0]
    value_tiles = tiled[1]
    query_tiles = query_part.reshape(frames, own_rows, TILE_H, TILE_COLS, tile_w, head_dim)
    query_tiles = jnp.transpose(query_tiles, (1, 3, 0, 2, 4, 5)).reshape(
        own_rows * TILE_COLS, frames * TILE_H * tile_w, head_dim
    )
    layer = lax.axis_index("tm")
    group = lax.axis_index("rows") // slabs
    tile_rows = lax.axis_size("rows") * rows_dev // TILE_H
    first_tile = (layer * tile_rows + group * own_rows) * TILE_COLS
    lists = lax.dynamic_slice_in_dim(window_lists, first_tile, own_rows * TILE_COLS, 0)
    present = lists >= 0
    safe_ids = jnp.where(present, lists, 0)
    layer_of = safe_ids // (tile_rows * TILE_COLS)
    row_of = safe_ids // TILE_COLS % tile_rows
    col_of = safe_ids % TILE_COLS
    position = (
        (layer_of - layer + 1) * stack_rows + (row_of - group * own_rows + 1)
    ) * TILE_COLS + col_of
    position = jnp.where(present, position, 0)
    scale = head_dim ** (-0.5)

    def attend(inputs):
        query_tile, slot_row, present_row = inputs
        key_rows = jnp.take(key_tiles, slot_row, axis=0).reshape(-1, head_dim)
        value_rows = jnp.take(value_tiles, slot_row, axis=0).reshape(-1, head_dim)
        scores = (
            lax.dot_general(
                query_tile, key_rows, (((1,), (1,)), ((), ())), preferred_element_type=jnp.float32
            )
            * scale
        )
        allowed = jnp.repeat(present_row, query_tile.shape[0])
        scores = jnp.where(allowed[None, :], scores, -1e30)
        peak = jnp.max(scores, axis=1, keepdims=True)
        weights = jnp.exp(scores - peak)
        total = jnp.sum(weights, axis=1, keepdims=True)
        mixed = jnp.dot(
            weights.astype(jnp.bfloat16), value_rows, preferred_element_type=jnp.float32
        )
        return (mixed / total).astype(jnp.bfloat16)

    result = lax.map(attend, (query_tiles, position, present))
    result = result.reshape(own_rows, TILE_COLS, frames, TILE_H, tile_w, head_dim)
    result = jnp.transpose(result, (2, 0, 3, 1, 4, 5)).reshape(
        frames, slabs, rows_dev, width, head_dim
    )
    result = jnp.transpose(result, (1, 0, 2, 3, 4))[None]
    merged = merge_heads(result)[:, 0]
    return jnp.transpose(merged, (1, 2, 3, 0, 4)).reshape(frames, rows_dev, width, feat)


def solution(mesh):
    return jax.shard_map(
        body,
        mesh=mesh,
        in_specs=(
            P("tm", "rows", None, None),
            P("tm", "rows", None, None),
            P("tm", "rows", None, None),
            P(),
        ),
        out_specs=P("tm", "rows", None, None),
        check_vma=False,
    )
```

profile of v0, /device:TPU:25, one launch (start us, length us, event | category | flops | bytes accessed | tf_op | source)
XLA Modules:
  0.0 388.6 jit_solution(3634098999345564731)
XLA Ops:
  0.0 1.4 copy.47
  4.5 2.7 collective-permute-done
  8.4 26.7 %collective-permute-done.1 = bf16[2,2,3,2,2,96,128]{6,5,4,3,2,1,0:T(8,128)(2,1)S(1)} collective-permute-done((bf16[2,2,3,2,2,96,128]{6,5,4,3,2,1,0:T(8,128)(2,1)S(1)}, bf16[2,2,3,2,2,96,128]{6,5,4,3,2,1,0:T(8,128)(2,1)S(1)}, u32[]{:S(2)}, u32[]{:S(2)}) %collective-permute-start.1) | collective-permute-done | bytes 1179680 | tf_op jit(solution)/shard_map/ppermute | solution.py:12
  36.2 1.4 broadcast_select_fusion.2
  38.8 1.6 collective-permute-start.2
  40.4 25.2 %collective-permute-done.2 = bf16[1,4,3,2,2,96,128]{6,5,4,3,2,1,0:T(8,128)(2,1)S(1)} collective-permute-done((bf16[1,4,3,2,2,96,128]{6,5,4,3,2,1,0:T(8,128)(2,1)}, bf16[1,4,3,2,2,96,128]{6,5,4,3,2,1,0:T(8,128)(2,1)S(1)}, u32[]{:S(2)}, u32[]{:S(2)}) %collective-permute-start.2) | collective-permute-done | bytes 1179680 | tf_op jit(solution)/shard_map/ppermute | solution.py:12
  66.1 1.3 copy-done.2
  67.6 4.9 %collective-permute-start.3 = (bf16[2,2,8,96,128]{4,3,2,1,0:T(8,128)(2,1)S(1)}, bf16[2,2,8,96,128]{4,3,2,1,0:T(8,128)(2,1)S(1)}, u32[]{:S(2)}, u32[]{:S(2)}) collective-permute-start(bf16[2,2,8,96,128]{4,3,2,1,0:T(8,128)(2,1)S(1)} %get-tuple-element.74), channel_id=1, source_target_pairs={{0,8},{1,9},{2,10},{3,11},{4,12},{5,13},{6,14},{7,15},{8,16},{9,17... | collective-permute-start | bytes 2359304 | tf_op jit(solution)/shard_map/ppermute | solution.py:18
  72.6 1.3 collective-permute-start.4
  73.9 13.6 %collective-permute-done.3 = bf16[2,2,8,96,128]{4,3,2,1,0:T(8,128)(2,1)S(1)} collective-permute-done((bf16[2,2,8,96,128]{4,3,2,1,0:T(8,128)(2,1)S(1)}, bf16[2,2,8,96,128]{4,3,2,1,0:T(8,128)(2,1)S(1)}, u32[]{:S(2)}, u32[]{:S(2)}) %collective-permute-start.3) | collective-permute-done | bytes 786464 | tf_op jit(solution)/shard_map/ppermute | solution.py:18
  87.5 25.1 %collective-permute-done.4 = bf16[2,2,8,96,128]{4,3,2,1,0:T(8,128)(2,1)S(1)} collective-permute-done((bf16[2,2,8,96,128]{4,3,2,1,0:T(8,128)(2,1)S(1)}, bf16[2,2,8,96,128]{4,3,2,1,0:T(8,128)(2,1)S(1)}, u32[]{:S(2)}, u32[]{:S(2)}) %collective-permute-start.4) | collective-permute-done | bytes 786464 | tf_op jit(solution)/shard_map/ppermute | solution.py:18
  113.0 2.9 collective-permute-start.6
  115.9 5.0 %collective-permute-start.5 = (bf16[2,2,32,96,128]{4,3,2,1,0:T(8,128)(2,1)S(1)}, bf16[2,2,32,96,128]{4,3,2,1,0:T(8,128)(2,1)}, u32[]{:S(2)}, u32[]{:S(2)}) collective-permute-start(bf16[2,2,32,96,128]{4,3,2,1,0:T(8,128)(2,1)S(1)} %pad_maximum_fusion), channel_id=1, source_target_pairs={{0,32},{32,64},{64,96},{96,128},{128,160},{160,192},{192,224},{1,3... | collective-permute-start | bytes 9437192 | tf_op jit(solution)/shard_map/ppermute | solution.py:18
  123.3 62.7 %collective-permute-done.6 = bf16[2,2,32,96,128]{4,3,2,1,0:T(8,128)(2,1)} collective-permute-done((bf16[2,2,32,96,128]{4,3,2,1,0:T(8,128)(2,1)S(1)}, bf16[2,2,32,96,128]{4,3,2,1,0:T(8,128)(2,1)}, u32[]{:S(2)}, u32[]{:S(2)}) %collective-permute-start.6) | collective-permute-done | bytes 3145760 | tf_op jit(solution)/shard_map/ppermute | solution.py:18
  186.0 68.8 %collective-permute-done.5 = bf16[2,2,32,96,128]{4,3,2,1,0:T(8,128)(2,1)} collective-permute-done((bf16[2,2,32,96,128]{4,3,2,1,0:T(8,128)(2,1)S(1)}, bf16[2,2,32,96,128]{4,3,2,1,0:T(8,128)(2,1)}, u32[]{:S(2)}, u32[]{:S(2)}) %collective-permute-start.5) | collective-permute-done | bytes 3145760 | tf_op jit(solution)/shard_map/ppermute | solution.py:18
  254.9 7.0 %maximum_bitcast_fusion = bf16[2,3,4,4,2,8,24,128]{7,6,3,5,2,4,0,1:T(8,128)(2,1)} fusion(bf16[1,2,2,4,8,4,24,128]{7,6,5,4,3,2,1,0:T(8,128)(2,1)} %bitcast.22, bf16[1,2,2,4,8,4,24,128]{7,6,5,4,3,2,1,0:T(8,128)(2,1)S(1)} %bitcast.138, bf16[1,2,2,4,8,4,24,128]{7,6,5,4,3,2,1,0:T(8,128)(2,1)} %bitcast.20), kind=kLoop, calls=%fused_computation.24 | loop fusion | flops 9437184 | bytes 18874368 | tf_op jit(solution)/shard_map/transpose | solution.py:79
  261.8 5.4 %fusion.44 = (bf16[1,3,4,4,2,8,24,128]{7,6,3,5,2,4,0,1:T(8,128)(2,1)S(1)}, bf16[1,3,4,4,2,8,24,128]{7,6,3,5,2,4,0,1:T(8,128)(2,1)S(1)}) fusion(bf16[2,3,4,4,2,8,24,128]{7,6,3,5,2,4,0,1:T(8,128)(2,1)} %maximum_bitcast_fusion), kind=kLoop, calls=%fused_computation.97 | loop fusion | bytes 18874368 | tf_op jit(solution)/shard_map/slice | solution.py:82
  267.2 3.5 copy.36
  270.7 3.4 copy.35
  274.2 89.2 %while.10 = (s32[]{:T(128)}, bf16[8,384,128]{2,1,0:T(8,128)(2,1)S(1)}, pred[8,12]{1,0:T(8,128)(4,1)S(1)}, bf16[8,384,128]{2,1,0:T(8,128)(2,1)}, s32[8,12]{1,0:T(...) while((s32[]{:T(128)}, bf16[8,384,128]{2,1,0:T(8,128)(2,1)S(1)}, ...), condition=%wide.region_3.5_spmd, body=%wide.region_0.4_spmd.sunk | while | flops 919634240 | bytes 33258392 | solution.py:123
  274.3 3.1 gather_fusion.1
  277.4 3.1 gather_fusion
  280.9 2.2 fusion.57
  285.5 3.1 gather_fusion.1
  288.6 3.1 gather_fusion
  292.0 2.2 fusion.57
  296.6 3.1 gather_fusion.1
  299.8 3.1 gather_fusion
  303.2 2.2 fusion.57
  307.8 3.1 gather_fusion.1
  310.9 3.1 gather_fusion
  314.3 2.2 fusion.57
  319.0 3.1 gather_fusion.1
  322.1 3.1 gather_fusion
  325.5 2.2 fusion.57
  330.1 3.1 gather_fusion.1
  333.2 3.1 gather_fusion
  336.6 2.2 fusion.57
  341.3 3.1 gather_fusion.1
  344.4 3.1 gather_fusion
  347.8 2.2 fusion.57
  352.4 3.1 gather_fusion.1
  355.6 3.1 gather_fusion
  359.0 2.2 fusion.57
  363.7 10.2 %collective-permute-done.7 = bf16[1,4,2,2,96,128]{5,4,3,2,1,0:T(8,128)(2,1)S(1)} collective-permute-done((bf16[1,4,2,2,96,128]{5,4,3,2,1,0:T(8,128)(2,1)S(1)}, bf16[1,4,2,2,96,128]{5,4,3,2,1,0:T(8,128)(2,1)S(1)}, u32[]{:S(2)}, u32[]{:S(2)}) %collective-permute-start.7) | collective-permute-done | bytes 393248 | tf_op jit(solution)/shard_map/ppermute | solution.py:12
  374.6 8.8 %collective-permute-done.8 = bf16[2,2,2,2,96,128]{5,4,3,2,1,0:T(8,128)(2,1)S(1)} collective-permute-done((bf16[2,2,2,2,96,128]{5,4,3,2,1,0:T(8,128)(2,1)S(1)}, bf16[2,2,2,2,96,128]{5,4,3,2,1,0:T(8,128)(2,1)S(1)}, u32[]{:S(2)}, u32[]{:S(2)}) %collective-permute-start.8) | collective-permute-done | bytes 393248 | tf_op jit(solution)/shard_map/ppermute | solution.py:12
  383.6 2.4 collective-permute-start.9
  386.0 1.3 collective-permute-done.9
  (119 shorter events, 33.8 us)
Async XLA Ops:
  0.0 120.9 %copy-start = (s32[256,12]{0,1:T(8,128)S(1)}, s32[256,12]{0,1:T(8,128)}, u32[]{:S(2)}) copy-start(s32[256,12]{0,1:T(8,128)} %param.11) | copy-start | bytes 36868
  0.0 1.4 copy-start.4
  0.0 1.6 copy-start.5
  3.8 3.4 collective-permute-start
  7.9 27.3 %collective-permute-start.1 = (bf16[2,2,3,2,2,96,128]{6,5,4,3,2,1,0:T(8,128)(2,1)S(1)}, bf16[2,2,3,2,2,96,128]{6,5,4,3,2,1,0:T(8,128)(2,1)S(1)}, u32[]{:S(2)}, u32[]{:S(2)}) collective-permute-start(bf16[2,2,3,2,2,96,128]{6,5,4,3,2,1,0:T(8,128)(2,1)S(1)} %bitcast.155), channel_id=1, source_target_pairs={{0,2},{1,3},{2,0},{3,1},{4,6},{5,7},{6,4},{7,5},{8,10},{9,11},{10,... | collective-permute-start | bytes 3538952 | tf_op jit(solution)/shard_map/ppermute | solution.py:12
  35.1 1.0 copy-start.3
  38.8 26.8 %collective-permute-start.2 = (bf16[1,4,3,2,2,96,128]{6,5,4,3,2,1,0:T(8,128)(2,1)}, bf16[1,4,3,2,2,96,128]{6,5,4,3,2,1,0:T(8,128)(2,1)S(1)}, u32[]{:S(2)}, u32[]{:S(2)}) collective-permute-start(bf16[1,4,3,2,2,96,128]{6,5,4,3,2,1,0:T(8,128)(2,1)} %fusion.22), channel_id=1, source_target_pairs={{0,4},{1,5},{2,6},{3,7},{4,0},{5,1},{6,2},{7,3},{8,12},{9,13},{10,... | collective-permute-start | bytes 3538952 | tf_op jit(solution)/shard_map/ppermute | solution.py:12
  66.0 1.4 copy-start.2
  67.6 19.9 %collective-permute-start.3 = (bf16[2,2,8,96,128]{4,3,2,1,0:T(8,128)(2,1)S(1)}, bf16[2,2,8,96,128]{4,3,2,1,0:T(8,128)(2,1)S(1)}, u32[]{:S(2)}, u32[]{:S(2)}) collective-permute-start(bf16[2,2,8,96,128]{4,3,2,1,0:T(8,128)(2,1)S(1)} %get-tuple-element.74), channel_id=1, source_target_pairs={{0,8},{1,9},{2,10},{3,11},{4,12},{5,13},{6,14},{7,15},{8,16},{9,17... | collective-permute-start | bytes 2359304 | tf_op jit(solution)/shard_map/ppermute | solution.py:18
  72.6 40.0 %collective-permute-start.4 = (bf16[2,2,8,96,128]{4,3,2,1,0:T(8,128)(2,1)S(1)}, bf16[2,2,8,96,128]{4,3,2,1,0:T(8,128)(2,1)S(1)}, u32[]{:S(2)}, u32[]{:S(2)}) collective-permute-start(bf16[2,2,8,96,128]{4,3,2,1,0:T(8,128)(2,1)S(1)} %get-tuple-element.75), channel_id=1, source_target_pairs={{8,0},{9,1},{10,2},{11,3},{12,4},{13,5},{14,6},{15,7},{16,8},{17,9... | collective-permute-start | bytes 2359304 | tf_op jit(solution)/shard_map/ppermute | solution.py:18
  113.0 73.0 %collective-permute-start.6 = (bf16[2,2,32,96,128]{4,3,2,1,0:T(8,128)(2,1)S(1)}, bf16[2,2,32,96,128]{4,3,2,1,0:T(8,128)(2,1)}, u32[]{:S(2)}, u32[]{:S(2)}) collective-permute-start(bf16[2,2,32,96,128]{4,3,2,1,0:T(8,128)(2,1)S(1)} %pad_maximum_fusion), channel_id=1, source_target_pairs={{32,0},{64,32},{96,64},{128,96},{160,128},{192,160},{224,192},{33,... | collective-permute-start | bytes 9437192 | tf_op jit(solution)/shard_map/ppermute | solution.py:18
  115.9 139.0 %collective-permute-start.5 = (bf16[2,2,32,96,128]{4,3,2,1,0:T(8,128)(2,1)S(1)}, bf16[2,2,32,96,128]{4,3,2,1,0:T(8,128)(2,1)}, u32[]{:S(2)}, u32[]{:S(2)}) collective-permute-start(bf16[2,2,32,96,128]{4,3,2,1,0:T(8,128)(2,1)S(1)} %pad_maximum_fusion), channel_id=1, source_target_pairs={{0,32},{32,64},{64,96},{96,128},{128,160},{160,192},{192,224},{1,3... | collective-permute-start | bytes 9437192 | tf_op jit(solution)/shard_map/ppermute | solution.py:18
  121.1 1.1 slice-start
  270.7 3.5 copy-start.6
  363.6 10.3 %collective-permute-start.7 = (bf16[1,4,2,2,96,128]{5,4,3,2,1,0:T(8,128)(2,1)S(1)}, bf16[1,4,2,2,96,128]{5,4,3,2,1,0:T(8,128)(2,1)S(1)}, u32[]{:S(2)}, u32[]{:S(2)}) collective-permute-start(bf16[1,4,2,2,96,128]{5,4,3,2,1,0:T(8,128)(2,1)S(1)} %bitcast.160), channel_id=1, source_target_pairs={{0,4},{1,5},{2,6},{3,7},{4,0},{5,1},{6,2},{7,3},{8,12},{9,13},{10,... | collective-permute-start | bytes 1179656 | tf_op jit(solution)/shard_map/ppermute | solution.py:12
  374.0 9.3 %collective-permute-start.8 = (bf16[2,2,2,2,96,128]{5,4,3,2,1,0:T(8,128)(2,1)S(1)}, bf16[2,2,2,2,96,128]{5,4,3,2,1,0:T(8,128)(2,1)S(1)}, u32[]{:S(2)}, u32[]{:S(2)}) collective-permute-start(bf16[2,2,2,2,96,128]{5,4,3,2,1,0:T(8,128)(2,1)S(1)} %fusion.25), channel_id=1, source_target_pairs={{0,2},{1,3},{2,0},{3,1},{4,6},{5,7},{6,4},{7,5},{8,10},{9,11},{10,... | collective-permute-start | bytes 1179656 | tf_op jit(solution)/shard_map/ppermute | solution.py:12
  383.6 3.7 collective-permute-start.9
  387.4 1.3 copy-start.1
where the time goes:
time: 390 us; the launch traced here: 389 us
  waiting for transfers between devices  245 us (63%)
  local copies, waits for them, and re-layouts  73.2 us (19%)
  matrix products  27 us (7%)
  other arithmetic  22.5 us (6%)
  starting transfers between devices  20 us (5%)
    ppermute x4, waiting for transfers between devices, shifted(): return lax.ppermute(block, axis, route)  170 us
    ppermute x6, waiting for transfers between devices, swapped(): lax.ppermute(shard, axis, [(i, i ^ 1 << bit) for i in range(lax.axis_size...  74.9 us
    gather x8, local copies, waits for them, and re-layouts, attend(): value_rows = jnp.take(value_tiles, slot_row, axis=0).reshape(-1, head_dim)  24.9 us
    gather x8, local copies, waits for them, and re-layouts, attend(): key_rows = jnp.take(key_tiles, slot_row, axis=0).reshape(-1, head_dim)  24.9 us
    dot_general x8, matrix products, attend(): lax.dot_general(query_tile, key_rows, (((1,), (1,)), ((), ())), preferred...  17.5 us
    ppermute x4, starting transfers between devices, shifted(): return lax.ppermute(block, axis, route)  14.1 us
    dot_general x8, matrix products, attend(): jnp.dot(weights.astype(jnp.bfloat16), value_rows, preferred_element_type=...  9.49 us
    slice x2, local copies, waits for them, and re-layouts, body(): value_tiles = tiled[1]  8.91 us
  transfers between devices with their start and end apart: 10, of which 10 were waited for; matrix products, arithmetic and copies ran while one was open for 0% of the time, Pallas kernels for 0%

commit v1 on v0

v1 whole, which is shorter than its diff:
```python
import functools

import jax
import jax.numpy as jnp
from jax import lax
from jax.experimental import pallas as pl
from jax.experimental.pallas import tpu as pltpu
from jax.sharding import PartitionSpec as P

HEADS = 8
COLS = 4
WIN = 12
TOK = 384
PART = 96
DIM = 128
LOG2E = 1.4426950408889634


def rc(src, dst, ss, rs, dev):
    return pltpu.make_async_remote_copy(
        src_ref=src, dst_ref=dst, send_sem=ss, recv_sem=rs, device_id=dev, device_id_type=pl.DeviceIdType.MESH
    )


def kernel(
    n_tm, n_rows, q_hbm, k_hbm, v_hbm, lists, out_hbm,
    qin, kin, vin, skv, sq, kv, qb, scores, ob, orecv, outv,
    in_sem, out_sem, kv_send, kv_recv, q_send, q_recv, z_send, z_recv, x_send, x_recv, o_send, o_recv, loc_sem,
):
    tm = lax.axis_index("tm")
    rows = lax.axis_index("rows")
    x, yh = tm // 2, tm % 2
    z, part = rows // 4, rows % 4
    me = yh * 4 + part

    def member(p):
        return (x * 2 + p // 4, z * 4 + p % 4)

    z_up = (tm, (rows + 4) % n_rows)
    z_dn = (tm, (rows + n_rows - 4) % n_rows)
    x_up = ((tm + 2) % n_tm, rows)
    x_dn = ((tm + n_tm - 2) % n_tm, rows)

    loads = [
        pltpu.make_async_copy(src, dst, in_sem.at[i])
        for i, (src, dst) in enumerate(((k_hbm, kin), (v_hbm, vin), (q_hbm, qin)))
    ]
    for c in loads:
        c.start()

    barrier = pltpu.get_barrier_semaphore()

    def greet(d, carry):
        pl.semaphore_signal(barrier, inc=1, device_id=member((me + d) % 8), device_id_type=pl.DeviceIdType.MESH)
        return carry

    lax.fori_loop(1, 8, greet, 0)
    for dev in (z_up, z_dn, x_up, x_dn):
        pl.semaphore_signal(barrier, inc=1, device_id=dev, device_id_type=pl.DeviceIdType.MESH)
    pl.semaphore_wait(barrier, 11)

    def pack(src, ct, p):
        feats = pl.ds(pl.multiple_of(p * DIM, DIM), DIM)
        pieces = []
        for f in range(2):
            for r in range(2):
                full = src[f, r, :, feats].astype(jnp.float32)
                pieces.append(full[ct * 24 : ct * 24 + 24])
        return jnp.concatenate(pieces, axis=0).astype(jnp.bfloat16)

    my_rows = pl.ds(pl.multiple_of(part * PART, PART), PART)

    def kv_piece(ct, d):
        p = (me + d) % 8
        return rc(
            skv.at[p, ct], kv.at[ct, 1 + yh, 1, :, my_rows], kv_send.at[ct, p], kv_recv.at[ct, me], member(p)
        )

    def kv_arrival(ct, p):
        return rc(
            skv.at[p, ct],
            kv.at[ct, 1 + p // 4, 1, :, pl.ds(pl.multiple_of((p % 4) * PART, PART), PART)],
            kv_send.at[ct, p], kv_recv.at[ct, p], member(p),
        )

    def q_piece(d):
        p = (me + d) % 8
        return rc(sq.at[p], qb.at[yh, :, my_rows], q_send.at[p], q_recv.at[me], member(p))

    def q_arrival(p):
        return rc(
            sq.at[p], qb.at[p // 4, :, pl.ds(pl.multiple_of((p % 4) * PART, PART), PART)],
            q_send.at[p], q_recv.at[p], member(p),
        )

    loads[0].wait()
    loads[1].wait()
    own_copies = []
    for ct in range(COLS):
        def send_kv(d, carry, ct=ct):
            p = (me + d) % 8
            skv[p, ct, 0] = pack(kin, ct, p)
            skv[p, ct, 1] = pack(vin, ct, p)
            kv_piece(ct, d).start()
            return carry

        lax.fori_loop(1, 8, send_kv, 0)
        skv[me, ct, 0] = pack(kin, ct, me)
        skv[me, ct, 1] = pack(vin, ct, me)
        own = pltpu.make_async_copy(skv.at[me, ct], kv.at[ct, 1 + yh, 1, :, my_rows], loc_sem.at[ct])
        own.start()
        own_copies.append(own)
    loads[2].wait()

    def send_q(d, carry):
        p = (me + d) % 8
        for ct in range(COLS):
            sq[p, ct] = pack(qin, ct, p)
        q_piece(d).start()
        return carry

    lax.fori_loop(1, 8, send_q, 0)
    for ct in range(COLS):
        sq[me, ct] = pack(qin, ct, me)
    own_q = pltpu.make_async_copy(sq.at[me], qb.at[yh, :, my_rows], loc_sem.at[COLS])
    own_q.start()

    def z_copy(ct, up, layer):
        dev = z_up if up else z_dn
        return rc(
            kv.at[ct, layer, 1], kv.at[ct, layer, 0 if up else 2],
            z_send.at[ct, up, layer], z_recv.at[ct, up, layer], dev,
        )

    def x_copy(ct, up, row):
        dev = x_up if up else x_dn
        return rc(
            kv.at[ct, 2 if up else 1, row], kv.at[ct, 0 if up else 3, row],
            x_send.at[ct, up, row], x_recv.at[ct, up, row], dev,
        )

    started = []

    def begin(c):
        c.start()
        started.append(c)

    for ct in range(COLS):
        own_copies[ct].wait()

        def take(d, carry, ct=ct):
            kv_arrival(ct, (me + d) % 8).wait_recv()
            return carry

        lax.fori_loop(1, 8, take, 0)
        for up in (1, 0):
            for layer in (1, 2):
                begin(z_copy(ct, up, layer))
            begin(x_copy(ct, up, 1))
    for ct in range(COLS):
        if ct < COLS - 1:
            for up in (1, 0):
                for layer in (1, 2):
                    z_copy(ct, up, layer).wait_recv()
            for up in (1, 0):
                for row in (0, 2):
                    begin(x_copy(ct, up, row))
        else:
            for up in (1, 0):
                x_copy(ct, up, 1).wait_recv()
            for up in (1, 0):
                for layer in (0, 3):
                    begin(z_copy(ct, up, layer))
    for ct in range(COLS):
        for up in (1, 0):
            if ct < COLS - 1:
                for row in (0, 1, 2):
                    x_copy(ct, up, row).wait_recv()
            else:
                for layer in (0, 1, 2, 3):
                    z_copy(ct, up, layer).wait_recv()
    own_q.wait()

    def take_q(d, carry):
        q_arrival((me + d) % 8).wait_recv()
        return carry

    lax.fori_loop(1, 8, take_q, 0)

    scale = DIM ** -0.5 * LOG2E
    ones = jnp.ones((TOK, DIM), jnp.bfloat16)

    def o_piece(i, s):
        layer, ct = i % 2, i // 2
        p = layer * 4 + s
        return rc(
            ob.at[layer, ct, pl.ds(s * PART, PART)], orecv.at[me, ct], o_send.at[i, s], o_recv.at[me, ct], member(p)
        )

    def own_o(ct):
        return pltpu.make_async_copy(ob.at[yh, ct, my_rows], orecv.at[me, ct], loc_sem.at[COLS + 1 + ct])

    def attend(i, carry):
        layer, ct = i % 2, i // 2
        tile = ((2 * x + layer) * 8 + z) * COLS + ct

        def place(slot):
            listed = lists[tile * WIN + slot]
            present = listed >= 0
            t = jnp.where(present, listed, tile)
            t_layer, t_row, t_col = t // 32, (t // 4) % 8, t % 4
            return t_col, jnp.clip(t_layer - 2 * x + 1, 0, 3), jnp.clip(t_row - z + 1, 0, 2), jnp.where(present, 1.0, 0.0)

        q = qb[layer, ct]
        peak = jnp.full((TOK, DIM), -jnp.inf, jnp.float32)
        for j in range(WIN // 2):
            keys = []
            for slot in (2 * j, 2 * j + 1):
                c_, l_, r_, _ = place(slot)
                keys.append(kv[c_, l_, r_, 0])
            s = lax.dot_general(
                q, jnp.concatenate(keys, axis=0), (((1,), (1,)), ((), ())), preferred_element_type=jnp.float32
            )
            scores[:, j * 2 * TOK : (j + 1) * 2 * TOK] = s
            for b in range(2 * TOK // DIM):
                peak = jnp.maximum(peak, s[:, b * DIM : (b + 1) * DIM])
        top = jnp.max(peak, axis=1, keepdims=True) * scale
        acc = jnp.zeros((TOK, 2 * DIM), jnp.float32)
        for j in range(WIN // 2):
            vals = []
            for slot in (2 * j, 2 * j + 1):
                c_, l_, r_, flag = place(slot)
                flag = jnp.full((TOK, DIM), flag, jnp.float32).astype(jnp.bfloat16)
                vals.append(jnp.concatenate((kv[c_, l_, r_, 1] * flag, ones * flag), axis=1))
            w = jnp.exp2(scores[:, j * 2 * TOK : (j + 1) * 2 * TOK] * scale - top).astype(jnp.bfloat16)
            acc = acc + jnp.dot(w, jnp.concatenate(vals, axis=0), preferred_element_type=jnp.float32)
        ob[layer, ct] = (acc[:, :DIM] / acc[:, DIM:]).astype(jnp.bfloat16)
        return carry

    def finish(i, carry):
        attend(i, carry)
        layer, ct = i % 2, i // 2
        for s in range(4):
            @pl.when(layer * 4 + s != me)
            def _():
                o_piece(i, s).start()

        @pl.when(layer == yh)
        def _():
            own_o(ct).start()

        return carry

    lax.fori_loop(0, 8, finish, 0)

    def drain(ct, carry):
        own_o(ct).wait()

        def take_o(d, c):
            p = (me + d) % 8
            rc(ob.at[yh, ct, my_rows], orecv.at[p, ct], o_send.at[0, 0], o_recv.at[p, ct], member(p)).wait_recv()
            return c

        lax.fori_loop(1, 8, take_o, 0)
        return carry

    lax.fori_loop(0, COLS, drain, 0)

    for h in range(HEADS):
        parts = [orecv[h, ct].astype(jnp.float32) for ct in range(COLS)]
        for f in range(2):
            for r in range(2):
                n = (2 * f + r) * 24
                row = jnp.concatenate([p_[n : n + 24] for p_ in parts], axis=0)
                outv[f, r, :, h * DIM : (h + 1) * DIM] = row.astype(jnp.bfloat16)
    done = pltpu.make_async_copy(outv, out_hbm, out_sem)
    done.start()

    def sent(d, carry):
        p = (me + d) % 8
        for ct in range(COLS):
            kv_piece(ct, d).wait_send()
        q_piece(d).wait_send()
        return carry

    lax.fori_loop(1, 8, sent, 0)
    for c in started:
        c.wait_send()

    def sent_o(i, carry):
        for s in range(4):
            @pl.when((i % 2) * 4 + s != me)
            def _():
                o_piece(i, s).wait_send()
        return carry

    lax.fori_loop(0, 8, sent_o, 0)
    done.wait()


def solution(mesh):
    n_tm, n_rows = mesh.shape["tm"], mesh.shape["rows"]
    bf = jnp.bfloat16
    vm = pltpu.VMEM
    dma = pltpu.SemaphoreType.DMA

    def body(queries, keys, values, window_lists):
        any_ = pl.BlockSpec(memory_space=pl.ANY)
        return pl.pallas_call(
            functools.partial(kernel, n_tm, n_rows),
            out_shape=jax.ShapeDtypeStruct(queries.shape, bf),
            in_specs=[any_, any_, any_, pl.BlockSpec(memory_space=pltpu.SMEM)],
            out_specs=any_,
            scratch_shapes=[
                vm(queries.shape, bf), vm(queries.shape, bf), vm(queries.shape, bf),
                vm((HEADS, COLS, 2, PART, DIM), bf),
                vm((HEADS, COLS, PART, DIM), bf),
                vm((COLS, 4, 3, 2, TOK, DIM), bf),
                vm((2, COLS, TOK, DIM), bf),
                vm((TOK, WIN * TOK), jnp.float32),
                vm((2, COLS, TOK, DIM), bf),
                vm((HEADS, COLS, PART, DIM), bf),
                vm(queries.shape, bf),
                dma((3,)), dma, dma((COLS, 8)), dma((COLS, 8)), dma((8,)), dma((8,)),
                dma((COLS, 2, 4)), dma((COLS, 2, 4)), dma((COLS, 2, 3)), dma((COLS, 2, 3)),
                dma((8, 4)), dma((8, COLS)), dma((2 * COLS + 1,)),
            ],
            compiler_params=pltpu.CompilerParams(
                collective_id=0, has_side_effects=True, vmem_limit_bytes=56 * 1024 * 1024
            ),
        )(queries, keys, values, window_lists.reshape(-1))

    row = P("tm", "rows", None, None)
    return jax.shard_map(body, mesh=mesh, in_specs=(row, row, row, P()), out_specs=row, check_vma=False)
```

time: 390 us -> 112 us (0.29)
  waiting for transfers between devices: 245 us -> 0 us
  Pallas kernels: 0 us -> 108 us
  local copies, waits for them, and re-layouts: 73.2 us -> 3.61 us
  matrix products: 27 us -> 0 us
  other arithmetic: 22.5 us -> 0 us
  starting transfers between devices: 20 us -> 0 us
    ppermute x10 -> x0, waiting for transfers between devices: 245 us -> none  [the longest x4 170 us: shifted(): return lax.ppermute(block, axis, route)]
    pallas_call x0 -> x1, Pallas kernels: none -> 108 us  [body(): pl.pallas_call(functools.partial(kernel, n_tm, n_rows), out_shape=jax.Sha...]
    gather x16 -> x0, local copies, waits for them, and re-layouts: 49.8 us -> none  [the longest x8 24.9 us: attend(): value_rows = jnp.take(value_tiles, slot_row, axis=0).reshape(-1, head_dim)]
    dot_general x16 -> x0, matrix products: 27 us -> none  [the longest x8 17.5 us: attend(): lax.dot_general(query_tile, key_rows, (((1,), (1,)), ((), ())), preferred...]
    ppermute x10 -> x0, starting transfers between devices: 20 us -> none  [the longest x4 14.1 us: shifted(): return lax.ppermute(block, axis, route)]
    slice x9 -> x0, local copies, waits for them, and re-layouts: 13.8 us -> none  [the longest x2 8.91 us: body(): value_tiles = tiled[1]]
    reduce_sum x8 -> x0, other arithmetic: 8.8 us -> none  [attend(): total = jnp.sum(weights, axis=1, keepdims=True)]
    transpose x3 -> x0, other arithmetic: 7.43 us -> none  [the longest x1 6.97 us: body(): tiled = jnp.transpose(tiled, (1, 0, 3, 5, 2, 4, 6, 7))]
  transfers between devices with their start and end apart: 10 -> 0, of which waited for: 10 -> 0; matrix products, arithmetic and copies ran while one was open for 0% -> 0% of each run, Pallas kernels for 0% -> 0%
where the time goes in v1:
time: 112 us
  Pallas kernels  108 us (96%)
  local copies, waits for them, and re-layouts  3.61 us (3%)
    pallas_call x1, Pallas kernels, body(): pl.pallas_call(functools.partial(kernel, n_tm, n_rows), out_shape=jax.Sha...  108 us
    unnamed x2, local copies, waits for them, and re-layouts  2.89 us

profile of v1, /device:TPU:25, one launch (start us, length us, event | category | flops | bytes accessed | tf_op | source)
XLA Modules:
  0.0 111.8 jit_solution(15516372910159582815)
XLA Ops:
  0.0 0.8 copy.5
  0.8 0.7 reshape.3.lists
  1.5 108.2 %shard_map.46 = bf16[2,2,96,1024]{3,2,1,0:T(8,128)(2,1)} custom-call(bf16[2,2,96,1024]{3,2,1,0:T(8,128)(2,1)} %q_hbm.1, bf16[2,2,96,1024]{3,2,1,0:T(8,128)(2,1)} %k_hbm.1, bf16[2,2,96,1024]{3,2,1,0:T(8,128)(2,1)} %v_hbm.1, s32[3072]{0:T(1024)} %reshape.3.lists), custom_call_target="tpu_custom_call" | custom-call | tf_op jit(solution)/shard_map/pallas_call | solution.py:309
  109.8 2.1 %copy.7 = bf16[2,2,96,1024]{3,2,1,0:T(8,128)(2,1)} copy(bf16[2,2,96,1024]{3,2,1,0:T(8,128)(2,1)} %shard_map.46) | data formatting | bytes 1572864

commit v2 on v1

--- a/solution.py
+++ b/solution.py
@@ -24,7 +24,7 @@
 
 def kernel(
     n_tm, n_rows, q_hbm, k_hbm, v_hbm, lists, out_hbm,
-    qin, kin, vin, skv, sq, kv, qb, scores, ob, orecv, outv,
+    qin, kin, vin, skv, sq, kv, qb, scores, peak, ob, orecv, outv,
     in_sem, out_sem, kv_send, kv_recv, q_send, q_recv, z_send, z_recv, x_send, x_recv, o_send, o_recv, loc_sem,
 ):
     tm = lax.axis_index("tm")
@@ -188,7 +188,6 @@
     lax.fori_loop(1, 8, take_q, 0)
 
     scale = DIM ** -0.5 * LOG2E
-    ones = jnp.ones((TOK, DIM), jnp.bfloat16)
 
     def o_piece(i, s):
         layer, ct = i % 2, i // 2
@@ -211,30 +210,37 @@
             t_layer, t_row, t_col = t // 32, (t // 4) % 8, t % 4
             return t_col, jnp.clip(t_layer - 2 * x + 1, 0, 3), jnp.clip(t_row - z + 1, 0, 2), jnp.where(present, 1.0, 0.0)
 
-        q = qb[layer, ct]
-        peak = jnp.full((TOK, DIM), -jnp.inf, jnp.float32)
-        for j in range(WIN // 2):
-            keys = []
-            for slot in (2 * j, 2 * j + 1):
-                c_, l_, r_, _ = place(slot)
-                keys.append(kv[c_, l_, r_, 0])
-            s = lax.dot_general(
-                q, jnp.concatenate(keys, axis=0), (((1,), (1,)), ((), ())), preferred_element_type=jnp.float32
-            )
-            scores[:, j * 2 * TOK : (j + 1) * 2 * TOK] = s
-            for b in range(2 * TOK // DIM):
-                peak = jnp.maximum(peak, s[:, b * DIM : (b + 1) * DIM])
-        top = jnp.max(peak, axis=1, keepdims=True) * scale
-        acc = jnp.zeros((TOK, 2 * DIM), jnp.float32)
-        for j in range(WIN // 2):
-            vals = []
-            for slot in (2 * j, 2 * j + 1):
-                c_, l_, r_, flag = place(slot)
-                flag = jnp.full((TOK, DIM), flag, jnp.float32).astype(jnp.bfloat16)
-                vals.append(jnp.concatenate((kv[c_, l_, r_, 1] * flag, ones * flag), axis=1))
-            w = jnp.exp2(scores[:, j * 2 * TOK : (j + 1) * 2 * TOK] * scale - top).astype(jnp.bfloat16)
-            acc = acc + jnp.dot(w, jnp.concatenate(vals, axis=0), preferred_element_type=jnp.float32)
-        ob[layer, ct] = (acc[:, :DIM] / acc[:, DIM:]).astype(jnp.bfloat16)
+        @pl.when(tm >= 0)
+        def _():
+            q = qb[layer, ct]
+            high = jnp.full((TOK, DIM), -jnp.inf, jnp.float32)
+            for j in range(WIN // 2):
+                keys = []
+                for slot in (2 * j, 2 * j + 1):
+                    c_, l_, r_, _ = place(slot)
+                    keys.append(kv[c_, l_, r_, 0])
+                s = lax.dot_general(
+                    q, jnp.concatenate(keys, axis=0), (((1,), (1,)), ((), ())), preferred_element_type=jnp.float32
+                )
+                scores[j] = s
+                for b in range(2 * TOK // DIM):
+                    high = jnp.maximum(high, s[:, b * DIM : (b + 1) * DIM])
+            peak[...] = jnp.broadcast_to(jnp.max(high, axis=1, keepdims=True) * scale, (TOK, DIM))
+
+        @pl.when(rows >= 0)
+        def _():
+            top = jnp.concatenate([peak[...]] * (2 * TOK // DIM), axis=1)
+            acc = jnp.zeros((TOK, 2 * DIM), jnp.float32)
+            for j in range(WIN // 2):
+                vals = []
+                for slot in (2 * j, 2 * j + 1):
+                    c_, l_, r_, flag = place(slot)
+                    flag = jnp.full((TOK, DIM), flag, jnp.float32).astype(jnp.bfloat16)
+                    vals.append(jnp.concatenate((kv[c_, l_, r_, 1] * flag, flag), axis=1))
+                w = jnp.exp2(scores[j] * scale - top).astype(jnp.bfloat16)
+                acc = acc + jnp.dot(w, jnp.concatenate(vals, axis=0), preferred_element_type=jnp.float32)
+            ob[layer, ct] = (acc[:, :DIM] / acc[:, DIM:]).astype(jnp.bfloat16)
+
         return carry
 
     def finish(i, carry):
@@ -317,7 +323,8 @@
                 vm((HEADS, COLS, PART, DIM), bf),
                 vm((COLS, 4, 3, 2, TOK, DIM), bf),
                 vm((2, COLS, TOK, DIM), bf),
-                vm((TOK, WIN * TOK), jnp.float32),
+                vm((WIN // 2, TOK, 2 * TOK), jnp.float32),
+                vm((TOK, DIM), jnp.float32),
                 vm((2, COLS, TOK, DIM), bf),
                 vm((HEADS, COLS, PART, DIM), bf),
                 vm(queries.shape, bf),

time: 112 us -> 90.2 us (0.81)
  Pallas kernels: 108 us -> 86.3 us
    pallas_call x1, Pallas kernels: 108 us -> 86.3 us  [body(): pl.pallas_call(functools.partial(kernel, n_tm, n_rows), out_shape=jax.Sha...]
where the time goes in v2:
time: 90.2 us; the launch traced here: 89.9 us
  Pallas kernels  86.3 us (96%)
  local copies, waits for them, and re-layouts  3.61 us (4%)
    pallas_call x1, Pallas kernels, body(): pl.pallas_call(functools.partial(kernel, n_tm, n_rows), out_shape=jax.Sha...  86.3 us
    unnamed x2, local copies, waits for them, and re-layouts  2.89 us

profile of v2, /device:TPU:25, one launch (start us, length us, event | category | flops | bytes accessed | tf_op | source)
XLA Modules:
  0.0 89.9 jit_solution(9342624089016951396)
XLA Ops:
  0.0 0.8 copy.5
  0.8 0.7 reshape.3.lists
  1.5 86.3 %shard_map.46 = bf16[2,2,96,1024]{3,2,1,0:T(8,128)(2,1)} custom-call(bf16[2,2,96,1024]{3,2,1,0:T(8,128)(2,1)} %q_hbm.1, bf16[2,2,96,1024]{3,2,1,0:T(8,128)(2,1)} %k_hbm.1, bf16[2,2,96,1024]{3,2,1,0:T(8,128)(2,1)} %v_hbm.1, s32[3072]{0:T(1024)} %reshape.3.lists), custom_call_target="tpu_custom_call" | custom-call | tf_op jit(solution)/shard_map/pallas_call | solution.py:315
  87.8 2.1 %copy.7 = bf16[2,2,96,1024]{3,2,1,0:T(8,128)(2,1)} copy(bf16[2,2,96,1024]{3,2,1,0:T(8,128)(2,1)} %shard_map.46) | data formatting | bytes 1572864

commit v3 on v2

v3 whole, which is shorter than its diff:
```python
import functools

import jax
import jax.numpy as jnp
from jax import lax
from jax.experimental import pallas as pl
from jax.experimental.pallas import tpu as pltpu
from jax.sharding import PartitionSpec as P

HEADS = 8
COLS = 4
WIN = 12
TOK = 384
PART = 96
DIM = 128
LOG2E = 1.4426950408889634


def rc(src, dst, ss, rs, dev):
    return pltpu.make_async_remote_copy(
        src_ref=src, dst_ref=dst, send_sem=ss, recv_sem=rs, device_id=dev, device_id_type=pl.DeviceIdType.MESH
    )


def kernel(
    n_tm, n_rows, q_hbm, k_hbm, v_hbm, lists_hbm, out_hbm,
    lists, qin, kin, vin, skv, sq, kv01, kv2, kv3, qb, scores, peak, ob, orecv, outv,
    in_sem, out_sem, kv_send, kv_recv, q_send, q_recv, z_send, z_recv, x_send, x_recv,
    cx_send, cx_recv, cz_send, cz_recv, o_send, o_recv, loc_sem,
):
    tm = lax.axis_index("tm")
    rows = lax.axis_index("rows")
    x, yh = tm // 2, tm % 2
    z, part = rows // 4, rows % 4
    me = yh * 4 + part

    def member(p):
        return (x * 2 + p // 4, z * 4 + p % 4)

    z_up = (tm, (rows + 4) % n_rows)
    z_dn = (tm, (rows + n_rows - 4) % n_rows)
    x_up = ((tm + 2) % n_tm, rows)
    x_dn = ((tm + n_tm - 2) % n_tm, rows)

    loads = [
        pltpu.make_async_copy(src, dst, in_sem.at[i])
        for i, (src, dst) in enumerate(((k_hbm, kin), (v_hbm, vin), (q_hbm, qin), (lists_hbm, lists)))
    ]
    for c in loads:
        c.start()

    barrier = pltpu.get_barrier_semaphore()

    def greet(d, carry):
        pl.semaphore_signal(barrier, inc=1, device_id=member((me + d) % 8), device_id_type=pl.DeviceIdType.MESH)
        return carry

    lax.fori_loop(1, 8, greet, 0)
    for dev in (z_up, z_dn, x_up, x_dn):
        pl.semaphore_signal(barrier, inc=1, device_id=dev, device_id_type=pl.DeviceIdType.MESH)
    pl.semaphore_wait(barrier, 11)

    def pack(src, ct, p):
        feats = pl.ds(pl.multiple_of(p * DIM, DIM), DIM)
        pieces = []
        for f in range(2):
            for r in range(2):
                full = src[f, r, :, feats].astype(jnp.float32)
                pieces.append(full[ct * 24 : ct * 24 + 24])
        return jnp.concatenate(pieces, axis=0).astype(jnp.bfloat16)

    def rows_of(p):
        return pl.ds(pl.multiple_of((p % 4) * PART, PART), PART)

    my_rows = rows_of(me)

    def tile(ct, layer, row):
        return kv01.at[ct, layer, row] if ct < 2 else (kv2, kv3)[ct - 2].at[layer, row]

    def kv_piece(ct, p, source):
        return rc(
            skv.at[p, ct], tile(ct, 1 + source // 4, 1).at[:, rows_of(source)],
            kv_send.at[ct, p], kv_recv.at[ct, source], member(p),
        )

    def q_piece(p, source):
        return rc(
            sq.at[p], qb.at[source // 4, :, rows_of(source)], q_send.at[p], q_recv.at[source], member(p)
        )

    def z_piece(ct, up, p, packed=False):
        return rc(
            skv.at[p, ct] if packed else tile(ct, 1 + p // 4, 1).at[:, rows_of(p)],
            tile(ct, 1 + p // 4, 0 if up else 2).at[:, rows_of(p)],
            z_send.at[ct, up, p], z_recv.at[ct, up, p], z_up if up else z_dn,
        )

    def x_piece(ct, p, packed=False):
        late = p // 4
        dev = ((tm + 2 * late + n_tm - 2 * (1 - late)) % n_tm, rows)
        return rc(
            skv.at[p, ct] if packed else tile(ct, 1 + late, 1).at[:, rows_of(p)],
            tile(ct, 3 - 3 * late, 1).at[:, rows_of(p)],
            x_send.at[ct, p], x_recv.at[ct, p], dev,
        )

    def x_corner(ct, up, row):
        return rc(
            tile(ct, 2 if up else 1, row), tile(ct, 0 if up else 3, row),
            cx_send.at[ct, up, row // 2], cx_recv.at[ct, up, row // 2], x_up if up else x_dn,
        )

    def z_corner(ct, up):
        layer = 3 if up else 0
        return rc(
            tile(ct, layer, 1), tile(ct, layer, 0 if up else 2),
            cz_send.at[ct - 2, up], cz_recv.at[ct - 2, up], z_up if up else z_dn,
        )

    def x_corners(ct):
        return [x_corner(ct, up, row) for up, row in (((1, 0), (0, 2), (1, 2), (0, 0)) if ct < 2 else ((1, 0), (0, 2)))]

    def z_corners(ct):
        return [z_corner(ct, up) for up in (1, 0)]

    def own_copy(ct):
        return pltpu.make_async_copy(skv.at[me, ct], tile(ct, 1 + yh, 1).at[:, my_rows], loc_sem.at[ct])

    def each(first, f):
        def step(d, carry):
            f((me + d) % 2 + 2 * ((me // 2 + d // 2) % 2) + 4 * ((me // 4 + d // 4) % 2), d)
            return carry

        lax.fori_loop(first, 8, step, 0)

    def own_first(ct):
        skv[me, ct, 0] = pack(kin, ct, me)
        skv[me, ct, 1] = pack(vin, ct, me)
        own_copy(ct).start()
        for c in (z_piece(ct, 1, me, True), z_piece(ct, 0, me, True), x_piece(ct, me, True)):
            c.start()

    def send_kv(ct):
        def one(p, d):
            skv[p, ct, 0] = pack(kin, ct, p)
            skv[p, ct, 1] = pack(vin, ct, p)
            kv_piece(ct, p, me).start()

        each(1, one)

    def forward_z(ct):
        own_copy(ct).wait()

        def one(p, d):
            kv_piece(ct, p, p).wait_recv()
            z_piece(ct, 1, p).start()
            z_piece(ct, 0, p).start()
            if ct < 2:
                x_piece(ct, p).start()

        each(1, one)

    def forward_x(ct):
        each(1, lambda p, d: x_piece(ct, p).start())

    def arrived_z(ct):
        def one(p, d):
            z_piece(ct, 1, p).wait_recv()
            z_piece(ct, 0, p).wait_recv()

        each(0, one)

    def arrived_x(ct):
        each(0, lambda p, d: x_piece(ct, p).wait_recv())

    def begin(copies):
        for c in copies:
            c.start()

    def arrived(copies):
        for c in copies:
            c.wait_recv()

    scale = DIM ** -0.5 * LOG2E

    def o_piece(layer, ct, s):
        p = layer * 4 + s
        return rc(
            ob.at[layer, ct, pl.ds(s * PART, PART)], orecv.at[me, ct], o_send.at[ct, layer, s], o_recv.at[me, ct], member(p)
        )

    def own_o(ct):
        return pltpu.make_async_copy(ob.at[yh, ct, my_rows], orecv.at[me, ct], loc_sem.at[COLS + 1 + ct])

    def attend(layer, ct, reach):
        tile = ((2 * x + layer) * 8 + z) * COLS + ct

        def place(slot):
            listed = lists[slot, tile]
            present = listed >= 0
            t = jnp.where(present, listed, tile)
            t_layer, t_row, t_col = t // 32, (t // 4) % 8, t % 4
            return t_col, jnp.clip(t_layer - 2 * x + 1, 0, 3), jnp.clip(t_row - z + 1, 0, 2), jnp.where(present, 1.0, 0.0)

        def pick(c_, l_, r_, which):
            found = kv01[jnp.clip(c_, 0, 1), l_, r_, which]
            if reach > 1:
                found = jnp.where(c_ == 2, kv2[l_, r_, which], found)
            if reach > 2:
                found = jnp.where(c_ == 3, kv3[l_, r_, which], found)
            return found

        @pl.when(tm >= 0)
        def _():
            q = qb[layer, ct]
            high = jnp.full((TOK, DIM), -jnp.inf, jnp.float32)
            for j in range(WIN // 2):
                keys = []
                for slot in (2 * j, 2 * j + 1):
                    c_, l_, r_, _ = place(slot)
                    keys.append(pick(c_, l_, r_, 0))
                s = lax.dot_general(
                    q, jnp.concatenate(keys, axis=0), (((1,), (1,)), ((), ())), preferred_element_type=jnp.float32
                )
                scores[j] = s
                for b in range(2 * TOK // DIM):
                    high = jnp.maximum(high, s[:, b * DIM : (b + 1) * DIM])
            peak[...] = jnp.broadcast_to(jnp.max(high, axis=1, keepdims=True) * scale, (TOK, DIM))

        @pl.when(rows >= 0)
        def _():
            top = jnp.concatenate([peak[...]] * (2 * TOK // DIM), axis=1)
            acc = jnp.zeros((TOK, 2 * DIM), jnp.float32)
            for j in range(WIN // 2):
                vals = []
                for slot in (2 * j, 2 * j + 1):
                    c_, l_, r_, flag = place(slot)
                    flag = jnp.full((TOK, DIM), flag, jnp.float32).astype(jnp.bfloat16)
                    vals.append(jnp.concatenate((pick(c_, l_, r_, 1) * flag, flag), axis=1))
                w = jnp.exp2(scores[j] * scale - top).astype(jnp.bfloat16)
                acc = acc + jnp.dot(w, jnp.concatenate(vals, axis=0), preferred_element_type=jnp.float32)
            ob[layer, ct] = (acc[:, :DIM] / acc[:, DIM:]).astype(jnp.bfloat16)

    def finish(first, count, reach):
        def step(i, carry):
            layer, ct = i % 2, first + i // 2
            attend(layer, ct, reach)
            for s in range(4):
                @pl.when(layer * 4 + s != me)
                def _():
                    o_piece(layer, ct, s).start()

            @pl.when(layer == yh)
            def _():
                own_o(ct).start()

            return carry

        lax.fori_loop(0, 2 * count, step, 0)

    def own_q():
        return pltpu.make_async_copy(sq.at[me], qb.at[yh, :, my_rows], loc_sem.at[COLS])

    def send_q():
        def one(p, d):
            for ct in range(COLS):
                sq[p, ct] = pack(qin, ct, p)

            @pl.when(d > 0)
            def _():
                q_piece(p, me).start()

        each(0, one)
        own_q().start()

    loads[0].wait()
    loads[1].wait()
    own_first(0)
    send_kv(0)
    own_first(1)
    own_first(2)
    own_first(3)
    send_kv(1)
    forward_z(0)
    send_kv(2)
    forward_z(1)
    send_kv(3)
    loads[2].wait()
    send_q()
    arrived_z(0)
    begin(x_corners(0))
    forward_z(2)
    arrived_z(1)
    begin(x_corners(1))
    forward_x(2)
    forward_z(3)
    forward_x(3)
    arrived_z(2)
    begin(x_corners(2))
    own_q().wait()
    loads[3].wait()
    each(1, lambda p, d: q_piece(p, p).wait_recv())
    for ct in (0, 1):
        arrived_x(ct)
        arrived(x_corners(ct))
    arrived_x(2)
    begin(z_corners(2))
    finish(0, 1, 1)
    arrived_z(3)
    begin(x_corners(3))
    arrived_x(3)
    begin(z_corners(3))
    arrived(x_corners(2))
    arrived(z_corners(2))
    finish(1, 1, 2)
    arrived(x_corners(3))
    arrived(z_corners(3))
    finish(2, 2, 3)

    def drain(ct, carry):
        own_o(ct).wait()

        def take_o(p, d):
            rc(
                ob.at[yh, ct, my_rows], orecv.at[p, ct], o_send.at[ct, 0, 0], o_recv.at[p, ct], member(p)
            ).wait_recv()

        each(1, take_o)
        return carry

    lax.fori_loop(0, COLS, drain, 0)

    for h in range(HEADS):
        parts = [orecv[h, ct].astype(jnp.float32) for ct in range(COLS)]
        for f in range(2):
            for r in range(2):
                n = (2 * f + r) * 24
                row = jnp.concatenate([p_[n : n + 24] for p_ in parts], axis=0)
                outv[f, r, :, h * DIM : (h + 1) * DIM] = row.astype(jnp.bfloat16)
    done = pltpu.make_async_copy(outv, out_hbm, out_sem)
    done.start()

    def sent(p, d):
        for ct in range(COLS):
            @pl.when(d > 0)
            def _():
                kv_piece(ct, p, me).wait_send()

            z_piece(ct, 1, p).wait_send()
            z_piece(ct, 0, p).wait_send()
            x_piece(ct, p).wait_send()

        @pl.when(d > 0)
        def _():
            q_piece(p, me).wait_send()

    each(0, sent)
    for ct in range(COLS):
        for c in x_corners(ct) + (z_corners(ct) if ct > 1 else []):
            c.wait_send()

    def sent_o(i, carry):
        for s in range(4):
            @pl.when((i % 2) * 4 + s != me)
            def _():
                o_piece(i % 2, i // 2, s).wait_send()
        return carry

    lax.fori_loop(0, 8, sent_o, 0)
    done.wait()


def solution(mesh):
    n_tm, n_rows = mesh.shape["tm"], mesh.shape["rows"]
    bf = jnp.bfloat16
    vm = pltpu.VMEM
    dma = pltpu.SemaphoreType.DMA

    def body(queries, keys, values, window_lists):
        any_ = pl.BlockSpec(memory_space=pl.ANY)
        return pl.pallas_call(
            functools.partial(kernel, n_tm, n_rows),
            out_shape=jax.ShapeDtypeStruct(queries.shape, bf),
            in_specs=[any_, any_, any_, any_],
            out_specs=any_,
            scratch_shapes=[
                pltpu.SMEM(window_lists.shape[::-1], jnp.int32),
                vm(queries.shape, bf), vm(queries.shape, bf), vm(queries.shape, bf),
                vm((HEADS, COLS, 2, PART, DIM), bf),
                vm((HEADS, COLS, PART, DIM), bf),
                vm((2, 4, 3, 2, TOK, DIM), bf), vm((4, 3, 2, TOK, DIM), bf), vm((4, 3, 2, TOK, DIM), bf),
                vm((2, COLS, TOK, DIM), bf),
                vm((WIN // 2, TOK, 2 * TOK), jnp.float32),
                vm((TOK, DIM), jnp.float32),
                vm((2, COLS, TOK, DIM), bf),
                vm((HEADS, COLS, PART, DIM), bf),
                vm(queries.shape, bf),
                dma((4,)), dma, dma((COLS, 8)), dma((COLS, 8)), dma((8,)), dma((8,)),
                dma((COLS, 2, 8)), dma((COLS, 2, 8)), dma((COLS, 8)), dma((COLS, 8)),
                dma((COLS, 2, 2)), dma((COLS, 2, 2)), dma((2, 2)), dma((2, 2)),
                dma((COLS, 2, 4)), dma((8, COLS)), dma((2 * COLS + 1,)),
            ],
            compiler_params=pltpu.CompilerParams(
                collective_id=0, has_side_effects=True, vmem_limit_bytes=56 * 1024 * 1024
            ),
        )(queries, keys, values, window_lists.T)

    row = P("tm", "rows", None, None)
    return jax.shard_map(body, mesh=mesh, in_specs=(row, row, row, P()), out_specs=row, check_vma=False)
```

time: 90.2 us -> 80.7 us (0.89)
  Pallas kernels: 86.3 us -> 78.5 us
  local copies, waits for them, and re-layouts: 3.61 us -> 2.06 us
    pallas_call x1, Pallas kernels: 86.3 us -> 78.5 us  [body(): pl.pallas_call(functools.partial(kernel, n_tm, n_rows), out_shape=jax.Sha...]
    unnamed x2 -> x1, local copies, waits for them, and re-layouts: 2.89 us -> 2.06 us
where the time goes in v3:
time: 80.7 us; the launch traced here: 80.5 us
  Pallas kernels  78.5 us (97%)
  local copies, waits for them, and re-layouts  2.06 us (3%)
    pallas_call x1, Pallas kernels, body(): pl.pallas_call(functools.partial(kernel, n_tm, n_rows), out_shape=jax.Sha...  78.5 us
    unnamed x1, local copies, waits for them, and re-layouts  2.06 us

profile of v3, /device:TPU:25, one launch (start us, length us, event | category | flops | bytes accessed | tf_op | source)
XLA Modules:
  0.0 80.5 jit_solution(17788978370437111405)
XLA Ops:
  0.0 78.5 %shard_map.46 = bf16[2,2,96,1024]{3,2,1,0:T(8,128)(2,1)} custom-call(bf16[2,2,96,1024]{3,2,1,0:T(8,128)(2,1)} %q_hbm.1, bf16[2,2,96,1024]{3,2,1,0:T(8,128)(2,1)} %k_hbm.1, bf16[2,2,96,1024]{3,2,1,0:T(8,128)(2,1)} %v_hbm.1, s32[12,256]{1,0:T(8,128)} %bitcast.1), custom_call_target="tpu_custom_call" | custom-call | tf_op jit(solution)/shard_map/pallas_call | solution.py:381
  78.5 2.1 %copy.6 = bf16[2,2,96,1024]{3,2,1,0:T(8,128)(2,1)} copy(bf16[2,2,96,1024]{3,2,1,0:T(8,128)(2,1)} %shard_map.46) | data formatting | bytes 1572864

commit v4 on v3

--- a/solution.py
+++ b/solution.py
@@ -80,19 +80,19 @@
     def kv_piece(ct, p, source):
         return rc(
             skv.at[p, ct], tile(ct, 1 + source // 4, 1).at[:, rows_of(source)],
-            kv_send.at[ct, p], kv_recv.at[ct, source], member(p),
+            kv_send, kv_recv.at[ct, source], member(p),
         )
 
     def q_piece(p, source):
         return rc(
-            sq.at[p], qb.at[source // 4, :, rows_of(source)], q_send.at[p], q_recv.at[source], member(p)
+            sq.at[p], qb.at[source // 4, :, rows_of(source)], q_send, q_recv, member(p)
         )
 
     def z_piece(ct, up, p, packed=False):
         return rc(
             skv.at[p, ct] if packed else tile(ct, 1 + p // 4, 1).at[:, rows_of(p)],
             tile(ct, 1 + p // 4, 0 if up else 2).at[:, rows_of(p)],
-            z_send.at[ct, up, p], z_recv.at[ct, up, p], z_up if up else z_dn,
+            z_send, z_recv.at[ct, up], z_up if up else z_dn,
         )
 
     def x_piece(ct, p, packed=False):
@@ -101,20 +101,20 @@
         return rc(
             skv.at[p, ct] if packed else tile(ct, 1 + late, 1).at[:, rows_of(p)],
             tile(ct, 3 - 3 * late, 1).at[:, rows_of(p)],
-            x_send.at[ct, p], x_recv.at[ct, p], dev,
+            x_send, x_recv.at[ct, late], dev,
         )
 
     def x_corner(ct, up, row):
         return rc(
             tile(ct, 2 if up else 1, row), tile(ct, 0 if up else 3, row),
-            cx_send.at[ct, up, row // 2], cx_recv.at[ct, up, row // 2], x_up if up else x_dn,
+            cx_send, cx_recv.at[ct, up], x_up if up else x_dn,
         )
 
     def z_corner(ct, up):
         layer = 3 if up else 0
         return rc(
             tile(ct, layer, 1), tile(ct, layer, 0 if up else 2),
-            cz_send.at[ct - 2, up], cz_recv.at[ct - 2, up], z_up if up else z_dn,
+            cz_send, cz_recv.at[ct - 2, up], z_up if up else z_dn,
         )
 
     def x_corners(ct):
@@ -128,7 +128,7 @@
 
     def each(first, f):
         def step(d, carry):
-            f((me + d) % 2 + 2 * ((me // 2 + d // 2) % 2) + 4 * ((me // 4 + d // 4) % 2), d)
+            f((me + d) % 8, d)
             return carry
 
         lax.fori_loop(first, 8, step, 0)
@@ -141,37 +141,51 @@
             c.start()
 
     def send_kv(ct):
-        def one(p, d):
+        def one(p):
             skv[p, ct, 0] = pack(kin, ct, p)
             skv[p, ct, 1] = pack(vin, ct, p)
             kv_piece(ct, p, me).start()
 
-        each(1, one)
-
-    def forward_z(ct):
+        return one
+
+    def forward_z(ct, x_too, following=None):
         own_copy(ct).wait()
 
-        def one(p, d):
+        def one(partner, d):
+            p = (me + 8 - d) % 8
             kv_piece(ct, p, p).wait_recv()
             z_piece(ct, 1, p).start()
             z_piece(ct, 0, p).start()
-            if ct < 2:
+            if x_too:
                 x_piece(ct, p).start()
+            if following is not None:
+                following(partner)
 
         each(1, one)
 
     def forward_x(ct):
         each(1, lambda p, d: x_piece(ct, p).start())
 
+    def landed(ref, sem):
+        rc(ref, ref, kv_send, sem, z_up).wait_recv()
+
+    def gone(ref, sem):
+        rc(ref, ref, sem, q_recv, z_up).wait_send()
+
+    def block(ct):
+        return kv01.at[ct] if ct < 2 else (kv2, kv3)[ct - 2]
+
     def arrived_z(ct):
-        def one(p, d):
-            z_piece(ct, 1, p).wait_recv()
-            z_piece(ct, 0, p).wait_recv()
-
-        each(0, one)
+        for up in (1, 0):
+            landed(block(ct).at[1:3, 0 if up else 2], z_recv.at[ct, up])
 
     def arrived_x(ct):
-        each(0, lambda p, d: x_piece(ct, p).wait_recv())
+        for late in (1, 0):
+            landed(tile(ct, 3 - 3 * late, 1), x_recv.at[ct, late])
+
+    def arrived_x_corners(ct):
+        for up in (1, 0):
+            landed(block(ct).at[0 if up else 3, 0 : (2 if ct < 2 else 1)], cx_recv.at[ct, up])
 
     def begin(copies):
         for c in copies:
@@ -186,11 +200,11 @@
     def o_piece(layer, ct, s):
         p = layer * 4 + s
         return rc(
-            ob.at[layer, ct, pl.ds(s * PART, PART)], orecv.at[me, ct], o_send.at[ct, layer, s], o_recv.at[me, ct], member(p)
+            ob.at[layer, ct, pl.ds(s * PART, PART)], orecv.at[me, ct], o_send, o_recv.at[ct], member(p)
         )
 
     def own_o(ct):
-        return pltpu.make_async_copy(ob.at[yh, ct, my_rows], orecv.at[me, ct], loc_sem.at[COLS + 1 + ct])
+        return pltpu.make_async_copy(ob.at[yh, ct, my_rows], orecv.at[me, ct], loc_sem.at[COLS + 1])
 
     def attend(layer, ct, reach):
         tile = ((2 * x + layer) * 8 + z) * COLS + ct
@@ -261,48 +275,41 @@
     def own_q():
         return pltpu.make_async_copy(sq.at[me], qb.at[yh, :, my_rows], loc_sem.at[COLS])
 
-    def send_q():
-        def one(p, d):
-            for ct in range(COLS):
-                sq[p, ct] = pack(qin, ct, p)
-
-            @pl.when(d > 0)
-            def _():
-                q_piece(p, me).start()
-
-        each(0, one)
-        own_q().start()
+    def pack_q(p):
+        for ct in range(COLS):
+            sq[p, ct] = pack(qin, ct, p)
+
+    def send_q(p):
+        pack_q(p)
+        q_piece(p, me).start()
 
     loads[0].wait()
     loads[1].wait()
     own_first(0)
-    send_kv(0)
+    each(1, lambda p, d: send_kv(0)(p))
     own_first(1)
+    forward_z(0, True, send_kv(1))
     own_first(2)
-    own_first(3)
-    send_kv(1)
-    forward_z(0)
-    send_kv(2)
-    forward_z(1)
-    send_kv(3)
-    loads[2].wait()
-    send_q()
+    forward_z(1, True, send_kv(2))
     arrived_z(0)
     begin(x_corners(0))
-    forward_z(2)
+    own_first(3)
+    forward_z(2, False, send_kv(3))
+    forward_x(2)
     arrived_z(1)
     begin(x_corners(1))
-    forward_x(2)
-    forward_z(3)
-    forward_x(3)
+    loads[2].wait()
+    forward_z(3, True, send_q)
+    pack_q(me)
+    own_q().start()
     arrived_z(2)
     begin(x_corners(2))
     own_q().wait()
     loads[3].wait()
-    each(1, lambda p, d: q_piece(p, p).wait_recv())
+    landed(sq.at[0:7], q_recv)
     for ct in (0, 1):
         arrived_x(ct)
-        arrived(x_corners(ct))
+        arrived_x_corners(ct)
     arrived_x(2)
     begin(z_corners(2))
     finish(0, 1, 1)
@@ -310,25 +317,16 @@
     begin(x_corners(3))
     arrived_x(3)
     begin(z_corners(3))
-    arrived(x_corners(2))
+    arrived_x_corners(2)
     arrived(z_corners(2))
     finish(1, 1, 2)
-    arrived(x_corners(3))
+    arrived_x_corners(3)
     arrived(z_corners(3))
     finish(2, 2, 3)
 
-    def drain(ct, carry):
-        own_o(ct).wait()
-
-        def take_o(p, d):
-            rc(
-                ob.at[yh, ct, my_rows], orecv.at[p, ct], o_send.at[ct, 0, 0], o_recv.at[p, ct], member(p)
-            ).wait_recv()
-
-        each(1, take_o)
-        return carry
-
-    lax.fori_loop(0, COLS, drain, 0)
+    pltpu.make_async_copy(orecv.at[me], orecv.at[me], loc_sem.at[COLS + 1]).wait()
+    for ct in range(COLS):
+        landed(orecv.at[0:7, ct], o_recv.at[ct])
 
     for h in range(HEADS):
         parts = [orecv[h, ct].astype(jnp.float32) for ct in range(COLS)]
@@ -340,33 +338,13 @@
     done = pltpu.make_async_copy(outv, out_hbm, out_sem)
     done.start()
 
-    def sent(p, d):
-        for ct in range(COLS):
-            @pl.when(d > 0)
-            def _():
-                kv_piece(ct, p, me).wait_send()
-
-            z_piece(ct, 1, p).wait_send()
-            z_piece(ct, 0, p).wait_send()
-            x_piece(ct, p).wait_send()
-
-        @pl.when(d > 0)
-        def _():
-            q_piece(p, me).wait_send()
-
-    each(0, sent)
-    for ct in range(COLS):
-        for c in x_corners(ct) + (z_corners(ct) if ct > 1 else []):
-            c.wait_send()
-
-    def sent_o(i, carry):
-        for s in range(4):
-            @pl.when((i % 2) * 4 + s != me)
-            def _():
-                o_piece(i % 2, i // 2, s).wait_send()
-        return carry
-
-    lax.fori_loop(0, 8, sent_o, 0)
+    gone(skv.at[0:7], kv_send)
+    gone(sq.at[0:7], q_send)
+    gone(kv01.at[:, :, 0:2], z_send)
+    gone(kv2.at[:, 0:2], x_send)
+    gone(kv01.at[0], cx_send)
+    gone(kv2.at[:, 0], cz_send)
+    gone(orecv.at[0:7], o_send)
     done.wait()
 
 
@@ -395,10 +373,8 @@
                 vm((2, COLS, TOK, DIM), bf),
                 vm((HEADS, COLS, PART, DIM), bf),
                 vm(queries.shape, bf),
-                dma((4,)), dma, dma((COLS, 8)), dma((COLS, 8)), dma((8,)), dma((8,)),
-                dma((COLS, 2, 8)), dma((COLS, 2, 8)), dma((COLS, 8)), dma((COLS, 8)),
-                dma((COLS, 2, 2)), dma((COLS, 2, 2)), dma((2, 2)), dma((2, 2)),
-                dma((COLS, 2, 4)), dma((8, COLS)), dma((2 * COLS + 1,)),
+                dma((4,)), dma, dma, dma((COLS, 8)), dma, dma, dma, dma((COLS, 2)), dma, dma((COLS, 2)),
+                dma, dma((COLS, 2)), dma, dma((2, 2)), dma, dma((COLS,)), dma((COLS + 2,)),
             ],
             compiler_params=pltpu.CompilerParams(
                 collective_id=0, has_side_effects=True, vmem_limit_bytes=56 * 1024 * 1024

time: 80.7 us -> 76.7 us (0.950)
  Pallas kernels: 78.5 us -> 74.5 us
    pallas_call x1, Pallas kernels: 78.5 us -> 74.5 us  [body(): pl.pallas_call(functools.partial(kernel, n_tm, n_rows), out_shape=jax.Sha...]
where the time goes in v4:
time: 76.7 us; the launch traced here: 76.6 us
  Pallas kernels  74.5 us (97%)
  local copies, waits for them, and re-layouts  2.06 us (3%)
    pallas_call x1, Pallas kernels, body(): pl.pallas_call(functools.partial(kernel, n_tm, n_rows), out_shape=jax.Sha...  74.5 us
    unnamed x1, local copies, waits for them, and re-layouts  2.06 us

profile of v4, /device:TPU:25, one launch (start us, length us, event | category | flops | bytes accessed | tf_op | source)
XLA Modules:
  0.0 76.6 jit_solution(812288117787668714)
XLA Ops:
  0.0 74.5 %shard_map.46 = bf16[2,2,96,1024]{3,2,1,0:T(8,128)(2,1)} custom-call(bf16[2,2,96,1024]{3,2,1,0:T(8,128)(2,1)} %q_hbm.1, bf16[2,2,96,1024]{3,2,1,0:T(8,128)(2,1)} %k_hbm.1, bf16[2,2,96,1024]{3,2,1,0:T(8,128)(2,1)} %v_hbm.1, s32[12,256]{1,0:T(8,128)} %bitcast.1), custom_call_target="tpu_custom_call" | custom-call | tf_op jit(solution)/shard_map/pallas_call | solution.py:359
  74.5 2.1 %copy.6 = bf16[2,2,96,1024]{3,2,1,0:T(8,128)(2,1)} copy(bf16[2,2,96,1024]{3,2,1,0:T(8,128)(2,1)} %shard_map.46) | data formatting | bytes 1572864

commit v5 on v4

--- a/solution.py
+++ b/solution.py
@@ -23,9 +23,9 @@
 
 
 def kernel(
-    n_tm, n_rows, q_hbm, k_hbm, v_hbm, lists_hbm, out_hbm,
-    lists, qin, kin, vin, skv, sq, kv01, kv2, kv3, qb, scores, peak, ob, orecv, outv,
-    in_sem, out_sem, kv_send, kv_recv, q_send, q_recv, z_send, z_recv, x_send, x_recv,
+    n_tm, n_rows, q_hbm, k_hbm, v_hbm, lists_hbm, out_ref,
+    lists, qin, kin, vin, skv, sq, kv01, kv2, kv3, far2, qb, scores, peak, held, held_peak, ob, orecv,
+    in_sem, kv_send, kv_recv, q_send, q_recv, z_send, z_recv, x_send, x_recv,
     cx_send, cx_recv, cz_send, cz_recv, o_send, o_recv, loc_sem,
 ):
     tm = lax.axis_index("tm")
@@ -75,6 +75,8 @@
     my_rows = rows_of(me)
 
     def tile(ct, layer, row):
+        if ct == 2 and not hasattr(layer, "dtype") and layer in (0, 3) and row != 1:
+            return far2.at[layer // 3, row // 2]
         return kv01.at[ct, layer, row] if ct < 2 else (kv2, kv3)[ct - 2].at[layer, row]
 
     def kv_piece(ct, p, source):
@@ -128,6 +130,7 @@
 
     def each(first, f):
         def step(d, carry):
+            d = d // 2 + 4 * (d % 2)
             f((me + d) % 8, d)
             return carry
 
@@ -185,7 +188,7 @@
 
     def arrived_x_corners(ct):
         for up in (1, 0):
-            landed(block(ct).at[0 if up else 3, 0 : (2 if ct < 2 else 1)], cx_recv.at[ct, up])
+            landed(kv01.at[0, 0 if up else 3, 0 : (2 if ct < 2 else 1)], cx_recv.at[ct, up])
 
     def begin(copies):
         for c in copies:
@@ -207,12 +210,15 @@
         return pltpu.make_async_copy(ob.at[yh, ct, my_rows], orecv.at[me, ct], loc_sem.at[COLS + 1])
 
     def attend(layer, ct, reach):
-        tile = ((2 * x + layer) * 8 + z) * COLS + ct
+        tile_id = ((2 * x + layer) * 8 + z) * COLS + ct
 
         def place(slot):
-            listed = lists[slot, tile]
+            listed = lists[slot, tile_id]
             present = listed >= 0
-            t = jnp.where(present, listed, tile)
+            if reach == 2:
+                f_layer, f_row, f_col = listed // 32, (listed // 4) % 8, listed % 4
+                present = present & ~far(f_col, f_layer - 2 * x + 1, f_row - z + 1)
+            t = jnp.where(present, listed, tile_id)
             t_layer, t_row, t_col = t // 32, (t // 4) % 8, t % 4
             return t_col, jnp.clip(t_layer - 2 * x + 1, 0, 3), jnp.clip(t_row - z + 1, 0, 2), jnp.where(present, 1.0, 0.0)
 
@@ -222,7 +228,11 @@
                 found = jnp.where(c_ == 2, kv2[l_, r_, which], found)
             if reach > 2:
                 found = jnp.where(c_ == 3, kv3[l_, r_, which], found)
+                found = jnp.where(far(c_, l_, r_), far2[l_ // 3, r_ // 2, which], found)
             return found
+
+        def far(c_, l_, r_):
+            return (c_ == 2) & ((l_ == 0) | (l_ == 3)) & (r_ != 1)
 
         @pl.when(tm >= 0)
         def _():
@@ -253,12 +263,58 @@
                     vals.append(jnp.concatenate((pick(c_, l_, r_, 1) * flag, flag), axis=1))
                 w = jnp.exp2(scores[j] * scale - top).astype(jnp.bfloat16)
                 acc = acc + jnp.dot(w, jnp.concatenate(vals, axis=0), preferred_element_type=jnp.float32)
+            if reach == 2:
+                held[layer] = acc
+                held_peak[layer] = peak[...]
+            else:
+                ob[layer, ct] = (acc[:, :DIM] / acc[:, DIM:]).astype(jnp.bfloat16)
+
+    def attend_far(layer, ct):
+        tile_id = ((2 * x + layer) * 8 + z) * COLS + ct
+        there = []
+        for row in (-1, 1):
+            corner = ((2 * x - 1 + 3 * layer) * 8 + z + row) * COLS + 2
+            hits = [jnp.where(lists[slot, tile_id] == corner, 1.0, 0.0) for slot in range(WIN)]
+            there.append(functools.reduce(jnp.maximum, hits))
+
+        @pl.when(tm >= 0)
+        def _():
+            keys = jnp.concatenate([far2[layer, row, 0] for row in (0, 1)], axis=0)
+            s = lax.dot_general(
+                qb[layer, ct], keys, (((1,), (1,)), ((), ())), preferred_element_type=jnp.float32
+            )
+            high = jnp.full((TOK, DIM), -1e30, jnp.float32)
+            for row in range(2):
+                part_s = s[:, row * TOK : (row + 1) * TOK] + (there[row] - 1.0) * 1e30
+                scores[0, :, row * TOK : (row + 1) * TOK] = part_s
+                for b in range(TOK // DIM):
+                    high = jnp.maximum(high, part_s[:, b * DIM : (b + 1) * DIM])
+            peak[...] = jnp.maximum(
+                held_peak[layer], jnp.broadcast_to(jnp.max(high, axis=1, keepdims=True) * scale, (TOK, DIM))
+            )
+
+        @pl.when(rows >= 0)
+        def _():
+            top = jnp.concatenate([peak[...]] * (2 * TOK // DIM), axis=1)
+            vals = []
+            for row in range(2):
+                flag = jnp.full((TOK, DIM), there[row], jnp.float32).astype(jnp.bfloat16)
+                vals.append(jnp.concatenate((far2[layer, row, 1] * flag, flag), axis=1))
+            w = jnp.exp2(scores[0] * scale - top).astype(jnp.bfloat16)
+            keep = jnp.exp2(held_peak[layer] - peak[...])
+            acc = held[layer] * jnp.concatenate((keep, keep), axis=1) + jnp.dot(
+                w, jnp.concatenate(vals, axis=0), preferred_element_type=jnp.float32
+            )
             ob[layer, ct] = (acc[:, :DIM] / acc[:, DIM:]).astype(jnp.bfloat16)
 
-    def finish(first, count, reach):
+    def hold(layer, carry):
+        attend(layer, 1, 2)
+        return carry
+
+    def finish(first, count, work):
         def step(i, carry):
             layer, ct = i % 2, first + i // 2
-            attend(layer, ct, reach)
+            work(layer, ct)
             for s in range(4):
                 @pl.when(layer * 4 + s != me)
                 def _():
@@ -295,9 +351,9 @@
     begin(x_corners(0))
     own_first(3)
     forward_z(2, False, send_kv(3))
-    forward_x(2)
     arrived_z(1)
     begin(x_corners(1))
+    forward_x(2)
     loads[2].wait()
     forward_z(3, True, send_q)
     pack_q(me)
@@ -310,19 +366,20 @@
     for ct in (0, 1):
         arrived_x(ct)
         arrived_x_corners(ct)
+    finish(0, 1, lambda layer, ct: attend(layer, ct, 1))
     arrived_x(2)
     begin(z_corners(2))
-    finish(0, 1, 1)
     arrived_z(3)
     begin(x_corners(3))
     arrived_x(3)
     begin(z_corners(3))
+    lax.fori_loop(0, 2, hold, 0)
     arrived_x_corners(2)
     arrived(z_corners(2))
-    finish(1, 1, 2)
+    finish(1, 1, attend_far)
     arrived_x_corners(3)
     arrived(z_corners(3))
-    finish(2, 2, 3)
+    finish(2, 2, lambda layer, ct: attend(layer, ct, 3))
 
     pltpu.make_async_copy(orecv.at[me], orecv.at[me], loc_sem.at[COLS + 1]).wait()
     for ct in range(COLS):
@@ -334,9 +391,7 @@
             for r in range(2):
                 n = (2 * f + r) * 24
                 row = jnp.concatenate([p_[n : n + 24] for p_ in parts], axis=0)
-                outv[f, r, :, h * DIM : (h + 1) * DIM] = row.astype(jnp.bfloat16)
-    done = pltpu.make_async_copy(outv, out_hbm, out_sem)
-    done.start()
+                out_ref[f, r, :, h * DIM : (h + 1) * DIM] = row.astype(jnp.bfloat16)
 
     gone(skv.at[0:7], kv_send)
     gone(sq.at[0:7], q_send)
@@ -345,7 +400,6 @@
     gone(kv01.at[0], cx_send)
     gone(kv2.at[:, 0], cz_send)
     gone(orecv.at[0:7], o_send)
-    done.wait()
 
 
 def solution(mesh):
@@ -360,24 +414,24 @@
             functools.partial(kernel, n_tm, n_rows),
             out_shape=jax.ShapeDtypeStruct(queries.shape, bf),
             in_specs=[any_, any_, any_, any_],
-            out_specs=any_,
+            out_specs=pl.BlockSpec(memory_space=pltpu.VMEM),
             scratch_shapes=[
                 pltpu.SMEM(window_lists.shape[::-1], jnp.int32),
                 vm(queries.shape, bf), vm(queries.shape, bf), vm(queries.shape, bf),
                 vm((HEADS, COLS, 2, PART, DIM), bf),
                 vm((HEADS, COLS, PART, DIM), bf),
                 vm((2, 4, 3, 2, TOK, DIM), bf), vm((4, 3, 2, TOK, DIM), bf), vm((4, 3, 2, TOK, DIM), bf),
+                vm((2, 2, 2, TOK, DIM), bf),
                 vm((2, COLS, TOK, DIM), bf),
                 vm((WIN // 2, TOK, 2 * TOK), jnp.float32),
-                vm((TOK, DIM), jnp.float32),
+                vm((TOK, DIM), jnp.float32), vm((2, TOK, 2 * DIM), jnp.float32), vm((2, TOK, DIM), jnp.float32),
                 vm((2, COLS, TOK, DIM), bf),
                 vm((HEADS, COLS, PART, DIM), bf),
-                vm(queries.shape, bf),
-                dma((4,)), dma, dma, dma((COLS, 8)), dma, dma, dma, dma((COLS, 2)), dma, dma((COLS, 2)),
+                dma((4,)), dma, dma((COLS, 8)), dma, dma, dma, dma((COLS, 2)), dma, dma((COLS, 2)),
                 dma, dma((COLS, 2)), dma, dma((2, 2)), dma, dma((COLS,)), dma((COLS + 2,)),
             ],
             compiler_params=pltpu.CompilerParams(
-                collective_id=0, has_side_effects=True, vmem_limit_bytes=56 * 1024 * 1024
+                collective_id=0, has_side_effects=True, vmem_limit_bytes=53 * 1024 * 1024
             ),
         )(queries, keys, values, window_lists.T)
 

time: 76.7 us -> 74.4 us (0.970)
  Pallas kernels: 74.5 us -> 72.7 us
    pallas_call x1, Pallas kernels: 74.5 us -> 72.7 us  [body(): pl.pallas_call(functools.partial(kernel, n_tm, n_rows), out_shape=jax.Sha...]
    unnamed x1 -> x3, local copies, waits for them, and re-layouts: 2.06 us -> 1.6 us
where the time goes in v5:
time: 74.4 us; the launch traced here: 74.3 us
  Pallas kernels  72.7 us (98%)
  local copies, waits for them, and re-layouts  1.6 us (2%)
    pallas_call x1, Pallas kernels, body(): pl.pallas_call(functools.partial(kernel, n_tm, n_rows), out_shape=jax.Sha...  72.7 us
    unnamed x3, local copies, waits for them, and re-layouts  1.6 us

profile of v5, /device:TPU:25, one launch (start us, length us, event | category | flops | bytes accessed | tf_op | source)
XLA Modules:
  0.0 74.3 jit_solution(7109493631849899752)
XLA Ops:
  0.0 0.0 copy-start
  0.0 0.7 copy-done
  0.7 72.7 %shard_map.46 = bf16[2,2,96,1024]{3,2,1,0:T(8,128)(2,1)S(1)} custom-call(bf16[2,2,96,1024]{3,2,1,0:T(8,128)(2,1)} %q_hbm.1, bf16[2,2,96,1024]{3,2,1,0:T(8,128)(2,1)} %k_hbm.1, bf16[2,2,96,1024]{3,2,1,0:T(8,128)(2,1)} %v_hbm.1, s32[12,256]{1,0:T(8,128)S(1)} %bitcast.1), custom_call_target="tpu_custom_call" | custom-call | tf_op jit(solution)/shard_map/pallas_call | solution.py:413
  73.4 0.9 %copy.6 = bf16[2,2,96,1024]{3,2,1,0:T(8,128)(2,1)} copy(bf16[2,2,96,1024]{3,2,1,0:T(8,128)(2,1)S(1)} %shard_map.46) | data formatting | bytes 1572864
Async XLA Ops:
  0.0 0.7 copy-start

commit v6 on v5

--- a/solution.py
+++ b/solution.py
@@ -223,8 +223,8 @@
             return t_col, jnp.clip(t_layer - 2 * x + 1, 0, 3), jnp.clip(t_row - z + 1, 0, 2), jnp.where(present, 1.0, 0.0)
 
         def pick(c_, l_, r_, which):
-            found = kv01[jnp.clip(c_, 0, 1), l_, r_, which]
-            if reach > 1:
+            found = kv2[l_, r_, which] if reach == 4 else kv01[jnp.clip(c_, 0, 1), l_, r_, which]
+            if 1 < reach < 4:
                 found = jnp.where(c_ == 2, kv2[l_, r_, which], found)
             if reach > 2:
                 found = jnp.where(c_ == 3, kv3[l_, r_, which], found)
@@ -351,13 +351,14 @@
     begin(x_corners(0))
     own_first(3)
     forward_z(2, False, send_kv(3))
+    loads[2].wait()
+    each(1, lambda p, d: send_q(p))
+    pack_q(me)
+    own_q().start()
     arrived_z(1)
     begin(x_corners(1))
     forward_x(2)
-    loads[2].wait()
-    forward_z(3, True, send_q)
-    pack_q(me)
-    own_q().start()
+    forward_z(3, True)
     arrived_z(2)
     begin(x_corners(2))
     own_q().wait()
@@ -379,7 +380,8 @@
     finish(1, 1, attend_far)
     arrived_x_corners(3)
     arrived(z_corners(3))
-    finish(2, 2, lambda layer, ct: attend(layer, ct, 3))
+    finish(2, 1, lambda layer, ct: attend(layer, ct, 3))
+    finish(3, 1, lambda layer, ct: attend(layer, ct, 4))
 
     pltpu.make_async_copy(orecv.at[me], orecv.at[me], loc_sem.at[COLS + 1]).wait()
     for ct in range(COLS):

time: 74.4 us -> 74.1 us (level)
  no operation moved by 1% of the time
where the time goes in v6:
time: 74.1 us; the launch traced here: 74 us
  Pallas kernels  72.4 us (98%)
  local copies, waits for them, and re-layouts  1.6 us (2%)
    pallas_call x1, Pallas kernels, body(): pl.pallas_call(functools.partial(kernel, n_tm, n_rows), out_shape=jax.Sha...  72.4 us
    unnamed x3, local copies, waits for them, and re-layouts  1.6 us

profile of v6, /device:TPU:25, one launch (start us, length us, event | category | flops | bytes accessed | tf_op | source)
XLA Modules:
  0.0 74.0 jit_solution(15015721157907761028)
XLA Ops:
  0.0 0.0 copy-start
  0.0 0.7 copy-done
  0.7 72.4 %shard_map.46 = bf16[2,2,96,1024]{3,2,1,0:T(8,128)(2,1)S(1)} custom-call(bf16[2,2,96,1024]{3,2,1,0:T(8,128)(2,1)} %q_hbm.1, bf16[2,2,96,1024]{3,2,1,0:T(8,128)(2,1)} %k_hbm.1, bf16[2,2,96,1024]{3,2,1,0:T(8,128)(2,1)} %v_hbm.1, s32[12,256]{1,0:T(8,128)S(1)} %bitcast.1), custom_call_target="tpu_custom_call" | custom-call | tf_op jit(solution)/shard_map/pallas_call | solution.py:415
  73.1 0.9 %copy.6 = bf16[2,2,96,1024]{3,2,1,0:T(8,128)(2,1)} copy(bf16[2,2,96,1024]{3,2,1,0:T(8,128)(2,1)S(1)} %shard_map.46) | data formatting | bytes 1572864
Async XLA Ops:
  0.0 0.7 copy-start

commit v7 on v6

--- a/solution.py
+++ b/solution.py
@@ -42,10 +42,11 @@
     x_up = ((tm + 2) % n_tm, rows)
     x_dn = ((tm + n_tm - 2) % n_tm, rows)
 
+    halves = [(k_hbm, kin, 0), (v_hbm, vin, 0), (k_hbm, kin, 48), (v_hbm, vin, 48)]
     loads = [
-        pltpu.make_async_copy(src, dst, in_sem.at[i])
-        for i, (src, dst) in enumerate(((k_hbm, kin), (v_hbm, vin), (q_hbm, qin), (lists_hbm, lists)))
-    ]
+        pltpu.make_async_copy(src.at[:, :, w : w + 48], dst.at[:, :, w : w + 48], in_sem.at[i])
+        for i, (src, dst, w) in enumerate(halves)
+    ] + [pltpu.make_async_copy(q_hbm, qin, in_sem.at[4]), pltpu.make_async_copy(lists_hbm, lists, in_sem.at[5])]
     for c in loads:
         c.start()
 
@@ -65,8 +66,8 @@
         pieces = []
         for f in range(2):
             for r in range(2):
-                full = src[f, r, :, feats].astype(jnp.float32)
-                pieces.append(full[ct * 24 : ct * 24 + 24])
+                half = src[f, r, ct // 2 * 48 : ct // 2 * 48 + 48, feats].astype(jnp.float32)
+                pieces.append(half[ct % 2 * 24 : ct % 2 * 24 + 24])
         return jnp.concatenate(pieces, axis=0).astype(jnp.bfloat16)
 
     def rows_of(p):
@@ -345,13 +346,15 @@
     each(1, lambda p, d: send_kv(0)(p))
     own_first(1)
     forward_z(0, True, send_kv(1))
+    loads[2].wait()
+    loads[3].wait()
     own_first(2)
     forward_z(1, True, send_kv(2))
     arrived_z(0)
     begin(x_corners(0))
     own_first(3)
     forward_z(2, False, send_kv(3))
-    loads[2].wait()
+    loads[4].wait()
     each(1, lambda p, d: send_q(p))
     pack_q(me)
     own_q().start()
@@ -362,7 +365,7 @@
     arrived_z(2)
     begin(x_corners(2))
     own_q().wait()
-    loads[3].wait()
+    loads[5].wait()
     landed(sq.at[0:7], q_recv)
     for ct in (0, 1):
         arrived_x(ct)
@@ -429,7 +432,7 @@
                 vm((TOK, DIM), jnp.float32), vm((2, TOK, 2 * DIM), jnp.float32), vm((2, TOK, DIM), jnp.float32),
                 vm((2, COLS, TOK, DIM), bf),
                 vm((HEADS, COLS, PART, DIM), bf),
-                dma((4,)), dma, dma((COLS, 8)), dma, dma, dma, dma((COLS, 2)), dma, dma((COLS, 2)),
+                dma((6,)), dma, dma((COLS, 8)), dma, dma, dma, dma((COLS, 2)), dma, dma((COLS, 2)),
                 dma, dma((COLS, 2)), dma, dma((2, 2)), dma, dma((COLS,)), dma((COLS + 2,)),
             ],
             compiler_params=pltpu.CompilerParams(

time: 74.1 us -> 74.2 us (level)
  no operation moved by 1% of the time
where the time goes in v7:
time: 74.2 us; the launch traced here: 74.1 us
  Pallas kernels  72.4 us (98%)
  local copies, waits for them, and re-layouts  1.6 us (2%)
    pallas_call x1, Pallas kernels, body(): pl.pallas_call(functools.partial(kernel, n_tm, n_rows), out_shape=jax.Sha...  72.4 us
    unnamed x3, local copies, waits for them, and re-layouts  1.6 us

profile of v7, /device:TPU:25, one launch (start us, length us, event | category | flops | bytes accessed | tf_op | source)
XLA Modules:
  0.0 74.1 jit_solution(9964574689535149769)
XLA Ops:
  0.0 0.0 copy-start
  0.0 0.7 copy-done
  0.7 72.4 %shard_map.46 = bf16[2,2,96,1024]{3,2,1,0:T(8,128)(2,1)S(1)} custom-call(bf16[2,2,96,1024]{3,2,1,0:T(8,128)(2,1)} %q_hbm.1, bf16[2,2,96,1024]{3,2,1,0:T(8,128)(2,1)} %k_hbm.1, bf16[2,2,96,1024]{3,2,1,0:T(8,128)(2,1)} %v_hbm.1, s32[12,256]{1,0:T(8,128)S(1)} %bitcast.1), custom_call_target="tpu_custom_call" | custom-call | tf_op jit(solution)/shard_map/pallas_call | solution.py:418
  73.2 0.9 %copy.6 = bf16[2,2,96,1024]{3,2,1,0:T(8,128)(2,1)} copy(bf16[2,2,96,1024]{3,2,1,0:T(8,128)(2,1)S(1)} %shard_map.46) | data formatting | bytes 1572864
Async XLA Ops:
  0.0 0.7 copy-start
